TPU v7x, 128 devices: a whole 4x4x4 slice. The times are simulated.
128 devices in a mesh: dp: 16 (over x, y), red: 8 (over z, core).
Axes of the slice: x: 4, y: 4, z: 4, core: 2. Of those that a mesh axis runs over, the one named last changes fastest.
Arguments:
- frames: bfloat16 [2048, 48, 1536], P(('dp', 'red')), may hold values from -36 to 36
- cotangent: bfloat16 [2048, 48, 1536], P(('dp', 'red')), may hold values from -6 to 6
- w_in: bfloat16 [1536, 3072], P('red'), may hold values from -0.15625 to 0.15625
- kernel: float32 [31, 1536], replicated, may hold values from -1 to 1
- gain: float32 [1536], replicated, may hold values from 0.25 to 1.75
- lengths: int32 [2048], replicated, may hold values from 1 to 47, as said below
Outputs:
- module_output: bfloat16 [2048, 48, 1536], P(('dp', 'red'))
- frame_gradient: bfloat16 [2048, 48, 1536], P(('dp', 'red'))
- grad_w_in: float32 [1536, 3072], P('red')
- grad_kernel: float32 [31, 1536], replicated
- grad_gain: float32 [1536], replicated
Inputs may be any that keep to these rules, and one draw needn't show every extreme that they name: The slots of each device, in order, form 16 groups of 1 slots. The q-th slot of group j on the device with dp index i and red index r and the q-th slot of group j on the device with dp index (2 j + 1 - i) mod 16 and the same red index have lengths that sum to exactly 48. The slots of dp index 0 all hold at least three quarters of 48 frames, rounded up.
All inputs are finite; a program needn't handle non-finite values.
Results may differ from a plain program's by a relative error of at most 0.0054.
Values may be sent and summed in bfloat16 or wider, within the bound.
A program may use at most 128 MiB of HBM per device.

v0:
```python
import jax
import jax.numpy as jnp
from jax import lax
from jax.sharding import PartitionSpec as P

EPSILON = 1e-05


def normalize(widened_frames):
    center = widened_frames - jnp.mean(widened_frames, axis=-1, keepdims=True)
    inv_std = lax.rsqrt(jnp.mean(center * center, axis=-1, keepdims=True) + EPSILON)
    return (center * inv_std, inv_std)


def block_pass(frames, cotangent, valid_frame_mask, segment, weights, kernel, gain):
    row_count, length, model_width = frames.shape
    tap_count = kernel.shape[0]
    reach = tap_count // 2
    widened_frames = frames.astype(jnp.float32)
    normed, inv_std = normalize(widened_frames)
    scaled = (normed * gain).astype(jnp.bfloat16)
    flat_in = scaled.reshape(row_count * length, model_width)
    hidden = jnp.dot(flat_in, weights, preferred_element_type=jnp.float32)
    hidden = hidden.reshape(row_count, length, 2 * model_width)
    value_portion = hidden[..., :model_width]
    gate_sigmoid = jax.nn.sigmoid(hidden[..., model_width:])
    frame_validity = valid_frame_mask.astype(jnp.float32)[..., None]
    gated_linear_output = value_portion * gate_sigmoid * frame_validity
    padded = jnp.pad(gated_linear_output, ((0, 0), (reach, reach), (0, 0)))
    seg_pad = jnp.pad(segment, ((0, 0), (reach, reach)), constant_values=-1)
    convolved_frames = jnp.zeros_like(gated_linear_output)
    for offset in range(tap_count):
        window = padded[:, offset : offset + length]
        same_seg = (seg_pad[:, offset : offset + length] == segment).astype(jnp.float32)[..., None]
        convolved_frames = convolved_frames + kernel[offset] * (window * same_seg)
    swish_activation = jax.nn.sigmoid(convolved_frames)
    module_output = (
        (widened_frames + convolved_frames * swish_activation) * frame_validity
    ).astype(jnp.bfloat16)
    incoming_gradient = cotangent.astype(jnp.float32) * frame_validity
    grad_conv = incoming_gradient * (
        swish_activation * (1.0 + convolved_frames * (1.0 - swish_activation))
    )
    grad_pad = jnp.pad(grad_conv, ((0, 0), (reach, reach), (0, 0)))
    gated_linear_gradient = jnp.zeros_like(gated_linear_output)
    kernel_terms = []
    for offset in range(tap_count):
        window = padded[:, offset : offset + length]
        same_seg = (seg_pad[:, offset : offset + length] == segment).astype(jnp.float32)[..., None]
        kernel_terms.append(jnp.sum(grad_conv * window * same_seg, axis=(0, 1)))
        back_start = 2 * reach - offset
        back_same = (seg_pad[:, back_start : back_start + length] == segment).astype(jnp.float32)[
            ..., None
        ]
        gated_linear_gradient = gated_linear_gradient + kernel[offset] * (
            grad_pad[:, back_start : back_start + length] * back_same
        )
    gated_linear_gradient = gated_linear_gradient * frame_validity
    grad_hidden = jnp.concatenate(
        [
            gated_linear_gradient * gate_sigmoid,
            gated_linear_gradient * value_portion * gate_sigmoid * (1.0 - gate_sigmoid),
        ],
        axis=-1,
    ).astype(jnp.bfloat16)
    flat_grad = grad_hidden.reshape(row_count * length, 2 * model_width)
    grad_scaled = lax.dot_general(
        flat_grad, weights, (((1,), (1,)), ((), ())), preferred_element_type=jnp.float32
    )
    grad_scaled = grad_scaled.reshape(row_count, length, model_width)
    gain_term = jnp.sum(grad_scaled * normed, axis=(0, 1))
    grad_normed = grad_scaled * gain
    frame_gradient = incoming_gradient + inv_std * (
        grad_normed
        - jnp.mean(grad_normed, axis=-1, keepdims=True)
        - normed * jnp.mean(grad_normed * normed, axis=-1, keepdims=True)
    )
    frame_gradient = (frame_gradient * frame_validity).astype(jnp.bfloat16)
    return (module_output, frame_gradient, flat_in, flat_grad, jnp.stack(kernel_terms), gain_term)


def local(frames, cotangent, w_in, kernel, gain, lengths):
    dp_size = lax.axis_size("dp")
    red_size = lax.axis_size("red")
    dp_index = lax.axis_index("dp")
    red_index = lax.axis_index("red")
    local_utts, length, model_width = frames.shape
    weights = lax.all_gather(w_in, "red", axis=0, tiled=True)
    positions = jnp.arange(length, dtype=jnp.int32)
    by_owner = lengths.reshape(dp_size, red_size, local_utts)
    own_lengths = lax.dynamic_slice(by_owner, (dp_index, red_index, 0), (1, 1, local_utts)).reshape(
        local_utts
    )
    valid_frame_mask = positions[None, :] < own_lengths[:, None]
    segment = jnp.where(valid_frame_mask, 0, 1).astype(jnp.int32)
    module_output, frame_gradient, flat_in, flat_grad, kernel_part, gain_part = block_pass(
        frames, cotangent, valid_frame_mask, segment, weights, kernel, gain
    )
    grad_scale = lax.rsqrt(jnp.sum(lengths).astype(jnp.float32))
    block_rows = model_width // (dp_size * red_size)
    ordered = flat_in.reshape(-1, red_size, dp_size, block_rows)
    ordered = jnp.transpose(ordered, (0, 2, 1, 3)).reshape(-1, model_width)
    owned_rows = lax.psum_scatter(
        lax.dot_general(
            ordered, flat_grad, (((0,), (0,)), ((), ())), preferred_element_type=jnp.float32
        ),
        ("dp", "red"),
        scatter_dimension=0,
        tiled=True,
    )
    grad_weights = lax.all_gather(owned_rows, "dp", axis=0, tiled=True)
    kernel_total, gain_total = lax.psum((kernel_part, gain_part), ("dp", "red"))
    return (
        module_output,
        frame_gradient,
        grad_weights * grad_scale,
        kernel_total * grad_scale,
        gain_total * grad_scale,
    )


def solution(mesh):
    placed = (
        P(("dp", "red"), None, None),
        P(("dp", "red"), None, None),
        P("red", None),
        P(),
        P(),
        P(),
    )
    return jax.shard_map(
        local,
        mesh=mesh,
        in_specs=placed,
        out_specs=(
            P(("dp", "red"), None, None),
            P(("dp", "red"), None, None),
            P("red", None),
            P(),
            P(),
        ),
        check_vma=False,
    )
```

profile of v0, /device:TPU:1, one launch (start us, length us, event | category | flops | bytes accessed | tf_op | source)
XLA Modules:
  0.0 923.5 jit_solution(477016552205187638)
XLA Ops:
  8.0 0.8 reshape.138
  8.8 2.1 convert_reduce_fusion
  10.8 0.7 fusion.19
  12.2 2.2 fusion.11
  14.4 8.3 copy.13
  22.7 10.7 %reshape_reshape.3 = bf16[768,8,16,12]{0,3,2,1:T(8,128)(2,1)} reshape(bf16[16,48,1536]{1,0,2:T(8,128)(2,1)} %copy.13) | data formatting | bytes 4718592 | tf_op jit(solution)/shard_map/reshape;reshape | solution.py:101
  33.4 4.0 copy.14
  37.4 5.2 reshape.139
  43.8 23.9 %all-gather.4.cloned.1.call-done = bf16[1536,3072]{1,0:T(8,128)(2,1)} async-done(((bf16[192,3072]{1,0:T(8,128)(2,1)}), bf16[1536,3072]{1,0:T(8,128)(2,1)}) %all-gather.4.cloned.1.call-update) | async-done | bytes 9437200 | tf_op jit(solution)/shard_map/all_gather | solution.py:88
  67.7 10.8 %fusion.3 = f32[16,48,3072]{2,1,0:T(8,128)S(1)} fusion(bf16[16,48,1536]{2,1,0:T(8,128)(2,1)} %fusion.11, bf16[1536,3072]{1,0:T(8,128)(2,1)} %all-gather.4.cloned.1.call-done), kind=kOutput, calls=%fused_computation.62 | convolution fusion | flops 7247757312 | bytes 21233664 | tf_op jit(solution)/shard_map/dot_general | solution.py:23
  78.6 1.3 multiply_multiply_fusion.1
  79.9 2.7 copy-done.3
  82.6 49.2 %multiply_reduce_fusion = (f32[1536]{0:T(1024)}, f32[1536]{0:T(1024)}, f32[1536]{0:T(1024)}, f32[1536]{0:T(1024)}, f32[1536]{0:T(1024)}, /*index=5*/f32[1536]{0:...) fusion(f32[16,48,1536]{2,1,0:T(8,128)S(1)} %multiply_multiply_f, ...), kind=kLoop, calls=%fused_computation.186 | loop fusion | flops 150981120 | bytes 16856064 | tf_op jit(solution)/shard_map/reduce_sum | solution.py:50
  132.0 28.6 %multiply_convert_fusion.1 = (bf16[16,48,1536]{2,1,0:T(8,128)(2,1)S(1)}, f32[16,48,1536]{2,1,0:T(8,128)}) fusion(f32[16,48,3072]{2,1,0:T(8,128)} %copy-done.3, f32[16,48]{1,0:T(8,128)S(1)} %get-tuple-element.106, f32[16,48]{1,0:T(8,128)S(1)} %get-tuple-element.76, f32[1536]{0:T(1024)} %copy-done.57, f32[16,48]{1,0:T(8,128)S(1)} %get-tuple-element.77, ...), kind=kLoop, calls=%fused_computation.218 | loop fusion | flops 114425856 | bytes 16800768 | tf_op jit(solution)/shard_map/convert.4
  160.6 6.9 multiply_convert_fusion
  167.5 1.4 copy-done.7
  168.9 10.8 %fusion.119 = f32[1536,3072]{1,0:T(8,128)} fusion(bf16[768,1536]{0,1:T(8,128)(2,1)S(1)} %copy-done.8, bf16[768,1536]{1,0:T(8,128)(2,1)S(1)} %bitcast.24, bf16[768,1536]{1,0:T(8,128)(2,1)S(1)} %bitcast.23), kind=kOutput, calls=%fused_computation.182 | convolution fusion | flops 7257194496 | bytes 25952256 | tf_op jit(solution)/shard_map/dot_general | solution.py:104
  179.8 359.8 %fusion = f32[16,3072]{1,0:T(8,128)S(1)} fusion(f32[1536,3072]{1,0:T(8,128)} %fusion.119), kind=kCustom, calls=%all-reduce-scatter | all-reduce-scatter fusion | flops 6291457 | bytes 19070976
  539.6 1.3 collective-permute-start.30
  540.9 1.3 collective-permute-start.31
  542.2 1.3 collective-permute-start.29
  543.5 1.3 collective-permute-start.28
  544.9 1.3 collective-permute-start.27
  546.2 1.3 collective-permute-start.26
  547.5 1.3 collective-permute-start.25
  548.8 1.3 collective-permute-start.24
  550.2 1.3 collective-permute-start.23
  552.0 15.3 %collective-permute-start.22 = (f32[16,3072]{1,0:T(8,128)S(1)}, f32[16,3072]{1,0:T(8,128)S(1)}, u32[]{:S(2)}, u32[]{:S(2)}) collective-permute-start(f32[16,3072]{1,0:T(8,128)S(1)} %fusion), channel_id=1, source_target_pairs={{0,23},{1,24},{2,25},{3,26},{4,27},{5,28},{6,29},{7,30},{8,31},{9,... | collective-permute-start | bytes 589832
  567.3 6.4 collective-permute-start.21
  573.7 5.7 collective-permute-start.20
  579.4 8.4 collective-permute-start.19
  587.8 2.0 collective-permute-start.18
  589.8 5.9 collective-permute-start.17
  595.7 2.0 collective-permute-start.16
  597.7 3.8 collective-permute-start.15
  601.6 0.7 reduce_sum.337
  603.1 5.5 collective-permute-start.14
  608.6 12.3 %collective-permute-start.13 = (f32[16,3072]{1,0:T(8,128)S(1)}, f32[16,3072]{1,0:T(8,128)S(1)}, u32[]{:S(2)}, u32[]{:S(2)}) collective-permute-start(f32[16,3072]{1,0:T(8,128)S(1)} %fusion), channel_id=1, source_target_pairs={{0,14},{1,15},{2,16},{3,17},{4,18},{5,19},{6,20},{7,21},{8,22},{9,... | collective-permute-start | bytes 589832
  620.9 10.3 %collective-permute-start.12 = (f32[16,3072]{1,0:T(8,128)S(1)}, f32[16,3072]{1,0:T(8,128)S(1)}, u32[]{:S(2)}, u32[]{:S(2)}) collective-permute-start(f32[16,3072]{1,0:T(8,128)S(1)} %fusion), channel_id=1, source_target_pairs={{0,13},{1,14},{2,15},{3,16},{4,17},{5,18},{6,19},{7,20},{8,21},{9,... | collective-permute-start | bytes 589832
  631.2 14.7 %collective-permute-start.11 = (f32[16,3072]{1,0:T(8,128)S(1)}, f32[16,3072]{1,0:T(8,128)S(1)}, u32[]{:S(2)}, u32[]{:S(2)}) collective-permute-start(f32[16,3072]{1,0:T(8,128)S(1)} %fusion), channel_id=1, source_target_pairs={{0,12},{1,13},{2,14},{3,15},{4,16},{5,17},{6,18},{7,19},{8,20},{9,... | collective-permute-start | bytes 589832
  646.0 1.3 collective-permute-start.10
  647.3 26.0 %multiply_reduce_fusion.9 = (f32[1536]{0:T(1024)S(1)}, f32[1536]{0:T(1024)S(1)}, f32[1536]{0:T(1024)S(1)}, f32[1536]{0:T(1024)S(1)}, f32[1536]{0:T(1024)S(1)}, /...) fusion(f32[16,48,1536]{2,1,0:T(8,128)} %copy-done.1, f32[16,48,1536]{2,1,0:T(8,128)} %copy-done, ...), kind=kLoop, calls=%fused_computation.195 | loop fusion | flops 30657024 | bytes 9517056 | tf_op jit(solution)/shard_map/reduce_sum | solution.py:50
  673.3 1.3 collective-permute-start.9
  674.6 5.2 collective-permute-start.8
  679.9 1.9 collective-permute-start.7
  681.8 2.5 collective-permute-start.6
  685.1 2.7 collective-permute-start.5
  687.9 9.0 multiply_reduce_fusion.18
  697.0 6.7 collective-permute-start.4
  703.7 2.0 collective-permute-start.3
  705.7 4.6 collective-permute-start.2
  710.3 2.0 collective-permute-start.1
  712.9 2.1 collective-permute-start
  715.0 3.9 multiply_reduce_fusion.27
  719.5 2.7 stack.127
  722.4 84.8 %concatenate.17 = f32[524,3072]{1,0:T(8,128)} concatenate(f32[12,3072]{1,0:T(8,128)S(1)} %collective-permute-done.31, f32[16,3072]{1,0:T(8,128)S(1)} %collective-permute-done.30, f32[16,3072]{1,0:T(8,128)} %copy-done.9, f32[16,3072]{1,0:T(8,128)} %copy-done.10, f32[16,3072]{1,0:T(8,128)} %copy-done.11, f32[16,3072]{1,0:T(8,128)} %copy-done.12, f32[16,3072]{1,0:T(8,128)} %copy-done.13, ...), dimensions={0} | concatenate | bytes 12877824
  807.2 1.7 dynamic-slice_bitcast_fusion
  808.9 14.3 %fusion.18 = (f32[1536]{0:T(1024)S(1)}, f32[16,48]{1,0:T(8,128)S(1)}, f32[16,48]{1,0:T(8,128)S(1)}, f32[16,48,1536]{2,1,0:T(8,128)}) fusion(bf16[16,48,1536]{2,1,0:T(8,128)(2,1)S(1)} %copy-done.4, f32[16,48]{1,0:T(8,128)S(1)} %copy-done.60, f32[16,48]{1,0:T(8,128)S(1)} %copy-done.52, f32[1536]{0:T(1024)S(1)} %copy-done.62, ...), kind=kOutput, calls=%fused_computation.80 | convolution fusion | flops 7267808256 | bytes 21258240 | tf_op jit(solution)/shard_map/dot_general | solution.py:67
  823.2 63.9 %psum.15 = f32[1536]{0:T(1024)S(1)} all-reduce(f32[1536]{0:T(1024)S(1)} %get-tuple-element.36), channel_id=1, replica_groups=mesh['dp'=16,'red'=8] {'dp','red'}, use_global_device_ids=true, to_apply=%region_39.40 | all-reduce | flops 1536 | bytes 12288 | tf_op jit(solution)/shard_map/psum | solution.py:112
  887.7 7.8 fusion.17
  895.6 1.6 broadcast_multiply_fusion.1
  897.2 12.9 %all-gather.6.cloned.1.call-done = f32[16,12,3072]{2,1,0:T(8,128)} async-done(((f32[1,12,3072]{2,1,0:T(8,128)}), f32[16,12,3072]{2,1,0:T(8,128)}) %all-gather.6.cloned.1.call-update) | async-done | bytes 2359312 | tf_op jit(solution)/shard_map/all_gather | solution.py:111
  910.1 3.9 broadcast_multiply_fusion
  914.0 3.0 reshape.143
  (232 shorter events, 5.5 us)
Async XLA Ops:
  7.2 60.5 %all-gather.4.cloned.1.call-start = ((), (), s32[]{:S(2)}) async-start(), calls=%async_computation | async-start | bytes 10616832 | tf_op jit(solution)/shard_map/all_gather | solution.py:88
  7.9 887.6 %all-reduce.7.cloned.1.call-start = ((), (), s32[]{:S(2)}) async-start(), calls=%async_computation.1 | async-start | bytes 393216 | tf_op jit(solution)/shard_map/psum | solution.py:112
  43.5 88.4 %copy-start.42 = (f32[16,48]{1,0:T(8,128)}, f32[16,48]{1,0:T(8,128)S(1)}, u32[]{:S(2)}) copy-start(f32[16,48]{1,0:T(8,128)S(1)} %get-tuple-element.89) | copy-start | bytes 9220
  43.5 88.4 %copy-start.44 = (f32[16,48]{1,0:T(8,128)}, f32[16,48]{1,0:T(8,128)S(1)}, u32[]{:S(2)}) copy-start(f32[16,48]{1,0:T(8,128)S(1)} %get-tuple-element.90) | copy-start | bytes 9220
  43.5 88.4 %copy-start.45 = (f32[16,48]{1,0:T(8,128)}, f32[16,48]{1,0:T(8,128)S(1)}, u32[]{:S(2)}) copy-start(f32[16,48]{1,0:T(8,128)S(1)} %get-tuple-element.91) | copy-start | bytes 9220
  43.5 88.4 %copy-start.46 = (f32[16,48]{1,0:T(8,128)}, f32[16,48]{1,0:T(8,128)S(1)}, u32[]{:S(2)}) copy-start(f32[16,48]{1,0:T(8,128)S(1)} %get-tuple-element.92) | copy-start | bytes 9220
  43.5 88.4 %copy-start.47 = (f32[16,48]{1,0:T(8,128)}, f32[16,48]{1,0:T(8,128)S(1)}, u32[]{:S(2)}) copy-start(f32[16,48]{1,0:T(8,128)S(1)} %get-tuple-element.93) | copy-start | bytes 9220
  43.6 88.3 %copy-start.48 = (f32[16,48]{1,0:T(8,128)}, f32[16,48]{1,0:T(8,128)S(1)}, u32[]{:S(2)}) copy-start(f32[16,48]{1,0:T(8,128)S(1)} %get-tuple-element.94) | copy-start | bytes 9220
  43.6 88.3 %copy-start.49 = (f32[16,48]{1,0:T(8,128)}, f32[16,48]{1,0:T(8,128)S(1)}, u32[]{:S(2)}) copy-start(f32[16,48]{1,0:T(8,128)S(1)} %get-tuple-element.95) | copy-start | bytes 9220
  43.6 88.3 %copy-start.50 = (f32[16,48]{1,0:T(8,128)}, f32[16,48]{1,0:T(8,128)S(1)}, u32[]{:S(2)}) copy-start(f32[16,48]{1,0:T(8,128)S(1)} %get-tuple-element.96) | copy-start | bytes 9220
  43.7 88.2 %copy-start.30 = (f32[16,48]{1,0:T(8,128)}, f32[16,48]{1,0:T(8,128)S(1)}, u32[]{:S(2)}) copy-start(f32[16,48]{1,0:T(8,128)S(1)} %get-tuple-element.79) | copy-start | bytes 9220
  43.7 88.2 %copy-start.32 = (f32[16,48]{1,0:T(8,128)}, f32[16,48]{1,0:T(8,128)S(1)}, u32[]{:S(2)}) copy-start(f32[16,48]{1,0:T(8,128)S(1)} %get-tuple-element.80) | copy-start | bytes 9220
  43.8 88.2 %copy-start.34 = (f32[16,48]{1,0:T(8,128)}, f32[16,48]{1,0:T(8,128)S(1)}, u32[]{:S(2)}) copy-start(f32[16,48]{1,0:T(8,128)S(1)} %get-tuple-element.81) | copy-start | bytes 9220
  43.8 88.2 %copy-start.36 = (f32[16,48]{1,0:T(8,128)}, f32[16,48]{1,0:T(8,128)S(1)}, u32[]{:S(2)}) copy-start(f32[16,48]{1,0:T(8,128)S(1)} %get-tuple-element.82) | copy-start | bytes 9220
  43.8 88.2 %copy-start.38 = (f32[16,48]{1,0:T(8,128)}, f32[16,48]{1,0:T(8,128)S(1)}, u32[]{:S(2)}) copy-start(f32[16,48]{1,0:T(8,128)S(1)} %get-tuple-element.83) | copy-start | bytes 9220
  43.8 88.2 %copy-start.40 = (f32[16,48]{1,0:T(8,128)}, f32[16,48]{1,0:T(8,128)S(1)}, u32[]{:S(2)}) copy-start(f32[16,48]{1,0:T(8,128)S(1)} %get-tuple-element.84) | copy-start | bytes 9220
  179.7 421.8 %copy-start.72 = (s32[2048]{0:T(1024)S(1)}, s32[2048]{0:T(1024)}, u32[]{:S(2)}) copy-start(s32[2048]{0:T(1024)} %param.11) | copy-start | bytes 24580
  179.7 467.5 %copy-start.43 = (f32[16,48]{1,0:T(8,128)S(1)}, f32[16,48]{1,0:T(8,128)}, u32[]{:S(2)}) copy-start(f32[16,48]{1,0:T(8,128)} %copy-done.42) | copy-start | bytes 9220
  539.6 7.9 collective-permute-start.30
  540.9 5.2 collective-permute-start.31
  542.2 6.6 collective-permute-start.29
  543.5 6.6 collective-permute-start.28
  544.9 7.2 collective-permute-start.27
  546.2 21.1 %collective-permute-start.26 = (f32[16,3072]{1,0:T(8,128)S(1)}, f32[16,3072]{1,0:T(8,128)S(1)}, u32[]{:S(2)}, u32[]{:S(2)}) collective-permute-start(f32[16,3072]{1,0:T(8,128)S(1)} %fusion), channel_id=1, source_target_pairs={{0,27},{1,28},{2,29},{3,30},{4,31},{5,32},{6,33},{7,34},{8,35},{9,... | collective-permute-start | bytes 589832
  547.5 26.2 %collective-permute-start.25 = (f32[16,3072]{1,0:T(8,128)S(1)}, f32[16,3072]{1,0:T(8,128)S(1)}, u32[]{:S(2)}, u32[]{:S(2)}) collective-permute-start(f32[16,3072]{1,0:T(8,128)S(1)} %fusion), channel_id=1, source_target_pairs={{0,26},{1,27},{2,28},{3,29},{4,30},{5,31},{6,32},{7,33},{8,34},{9,... | collective-permute-start | bytes 589832
  548.8 30.6 %collective-permute-start.24 = (f32[16,3072]{1,0:T(8,128)S(1)}, f32[16,3072]{1,0:T(8,128)S(1)}, u32[]{:S(2)}, u32[]{:S(2)}) collective-permute-start(f32[16,3072]{1,0:T(8,128)S(1)} %fusion), channel_id=1, source_target_pairs={{0,25},{1,26},{2,27},{3,28},{4,29},{5,30},{6,31},{7,32},{8,33},{9,... | collective-permute-start | bytes 589832
  550.1 51.4 %copy-start.10 = (f32[16,3072]{1,0:T(8,128)}, f32[16,3072]{1,0:T(8,128)S(1)}, u32[]{:S(2)}) copy-start(f32[16,3072]{1,0:T(8,128)S(1)} %collective-permute-done.28) | copy-start | bytes 589828
  550.2 37.6 %collective-permute-start.23 = (f32[16,3072]{1,0:T(8,128)S(1)}, f32[16,3072]{1,0:T(8,128)S(1)}, u32[]{:S(2)}, u32[]{:S(2)}) collective-permute-start(f32[16,3072]{1,0:T(8,128)S(1)} %fusion), channel_id=1, source_target_pairs={{0,24},{1,25},{2,26},{3,27},{4,28},{5,29},{6,30},{7,31},{8,32},{9,... | collective-permute-start | bytes 589832
  552.0 49.5 %copy-start.11 = (f32[16,3072]{1,0:T(8,128)}, f32[16,3072]{1,0:T(8,128)S(1)}, u32[]{:S(2)}) copy-start(f32[16,3072]{1,0:T(8,128)S(1)} %collective-permute-done.27) | copy-start | bytes 589828
  552.0 37.8 %collective-permute-start.22 = (f32[16,3072]{1,0:T(8,128)S(1)}, f32[16,3072]{1,0:T(8,128)S(1)}, u32[]{:S(2)}, u32[]{:S(2)}) collective-permute-start(f32[16,3072]{1,0:T(8,128)S(1)} %fusion), channel_id=1, source_target_pairs={{0,23},{1,24},{2,25},{3,26},{4,27},{5,28},{6,29},{7,30},{8,31},{9,... | collective-permute-start | bytes 589832
  567.3 28.4 %collective-permute-start.21 = (f32[16,3072]{1,0:T(8,128)S(1)}, f32[16,3072]{1,0:T(8,128)S(1)}, u32[]{:S(2)}, u32[]{:S(2)}) collective-permute-start(f32[16,3072]{1,0:T(8,128)S(1)} %fusion), channel_id=1, source_target_pairs={{0,22},{1,23},{2,24},{3,25},{4,26},{5,27},{6,28},{7,29},{8,30},{9,... | collective-permute-start | bytes 589832
  573.7 24.0 %collective-permute-start.20 = (f32[16,3072]{1,0:T(8,128)S(1)}, f32[16,3072]{1,0:T(8,128)S(1)}, u32[]{:S(2)}, u32[]{:S(2)}) collective-permute-start(f32[16,3072]{1,0:T(8,128)S(1)} %fusion), channel_id=1, source_target_pairs={{0,21},{1,22},{2,23},{3,24},{4,25},{5,26},{6,27},{7,28},{8,29},{9,... | collective-permute-start | bytes 589832
  579.4 23.7 %collective-permute-start.19 = (f32[16,3072]{1,0:T(8,128)S(1)}, f32[16,3072]{1,0:T(8,128)}, u32[]{:S(2)}, u32[]{:S(2)}) collective-permute-start(f32[16,3072]{1,0:T(8,128)S(1)} %fusion), channel_id=1, source_target_pairs={{0,20},{1,21},{2,22},{3,23},{4,24},{5,25},{6,26},{7,27},{8,28},{9,... | collective-permute-start | bytes 589832
  587.8 20.8 %collective-permute-start.18 = (f32[16,3072]{1,0:T(8,128)S(1)}, f32[16,3072]{1,0:T(8,128)}, u32[]{:S(2)}, u32[]{:S(2)}) collective-permute-start(f32[16,3072]{1,0:T(8,128)S(1)} %fusion), channel_id=1, source_target_pairs={{0,19},{1,20},{2,21},{3,22},{4,23},{5,24},{6,25},{7,26},{8,27},{9,... | collective-permute-start | bytes 589832
  589.8 31.1 %collective-permute-start.17 = (f32[16,3072]{1,0:T(8,128)S(1)}, f32[16,3072]{1,0:T(8,128)}, u32[]{:S(2)}, u32[]{:S(2)}) collective-permute-start(f32[16,3072]{1,0:T(8,128)S(1)} %fusion), channel_id=1, source_target_pairs={{0,18},{1,19},{2,20},{3,21},{4,22},{5,23},{6,24},{7,25},{8,26},{9,... | collective-permute-start | bytes 589832
  595.7 35.5 %collective-permute-start.16 = (f32[16,3072]{1,0:T(8,128)S(1)}, f32[16,3072]{1,0:T(8,128)}, u32[]{:S(2)}, u32[]{:S(2)}) collective-permute-start(f32[16,3072]{1,0:T(8,128)S(1)} %fusion), channel_id=1, source_target_pairs={{0,17},{1,18},{2,19},{3,20},{4,21},{5,22},{6,23},{7,24},{8,25},{9,... | collective-permute-start | bytes 589832
  597.7 48.2 %collective-permute-start.15 = (f32[16,3072]{1,0:T(8,128)S(1)}, f32[16,3072]{1,0:T(8,128)}, u32[]{:S(2)}, u32[]{:S(2)}) collective-permute-start(f32[16,3072]{1,0:T(8,128)S(1)} %fusion), channel_id=1, source_target_pairs={{0,16},{1,17},{2,18},{3,19},{4,20},{5,21},{6,22},{7,23},{8,24},{9,... | collective-permute-start | bytes 589832
  603.0 84.8 %slice-start = ((s8[4718592]{0:T(1024)(128)(4,1)}), s8[524288]{0:T(1024)(128)(4,1)S(1)}, s32[]{:S(2)}) async-start(s8[4718592]{0:T(1024)(128)(4,1)} %bitcast.20), calls=%async_computation.3 | async-start | bytes 1048576
  603.1 84.7 %slice-start.1 = ((s8[4718592]{0:T(1024)(128)(4,1)}), s8[4194304]{0:T(1024)(128)(4,1)S(1)}, s32[]{:S(2)}) async-start(s8[4718592]{0:T(1024)(128)(4,1)} %bitcast.20), calls=%async_computation.4 | async-start | bytes 8388608
  603.1 84.7 %copy-start.2 = (f32[16,48,1536]{2,1,0:T(8,128)S(1)}, f32[16,48,1536]{2,1,0:T(8,128)}, u32[]{:S(2)}) copy-start(f32[16,48,1536]{2,1,0:T(8,128)} %copy-done.1) | copy-start | bytes 14155780
  603.1 84.7 %copy-start.33 = (f32[16,48]{1,0:T(8,128)S(1)}, f32[16,48]{1,0:T(8,128)}, u32[]{:S(2)}) copy-start(f32[16,48]{1,0:T(8,128)} %copy-done.32) | copy-start | bytes 9220
  603.1 84.7 %copy-start.35 = (f32[16,48]{1,0:T(8,128)S(1)}, f32[16,48]{1,0:T(8,128)}, u32[]{:S(2)}) copy-start(f32[16,48]{1,0:T(8,128)} %copy-done.34) | copy-start | bytes 9220
  603.1 84.7 %copy-start.37 = (f32[16,48]{1,0:T(8,128)S(1)}, f32[16,48]{1,0:T(8,128)}, u32[]{:S(2)}) copy-start(f32[16,48]{1,0:T(8,128)} %copy-done.36) | copy-start | bytes 9220
  603.1 84.7 %copy-start.39 = (f32[16,48]{1,0:T(8,128)S(1)}, f32[16,48]{1,0:T(8,128)}, u32[]{:S(2)}) copy-start(f32[16,48]{1,0:T(8,128)} %copy-done.38) | copy-start | bytes 9220
  603.1 84.7 %copy-start.41 = (f32[16,48]{1,0:T(8,128)S(1)}, f32[16,48]{1,0:T(8,128)}, u32[]{:S(2)}) copy-start(f32[16,48]{1,0:T(8,128)} %copy-done.40) | copy-start | bytes 9220
  603.1 70.1 %collective-permute-start.14 = (f32[16,3072]{1,0:T(8,128)S(1)}, f32[16,3072]{1,0:T(8,128)S(1)}, u32[]{:S(2)}, u32[]{:S(2)}) collective-permute-start(f32[16,3072]{1,0:T(8,128)S(1)} %fusion), channel_id=1, source_target_pairs={{0,15},{1,16},{2,17},{3,18},{4,19},{5,20},{6,21},{7,22},{8,23},{9,... | collective-permute-start | bytes 589832
  608.6 65.9 %collective-permute-start.13 = (f32[16,3072]{1,0:T(8,128)S(1)}, f32[16,3072]{1,0:T(8,128)S(1)}, u32[]{:S(2)}, u32[]{:S(2)}) collective-permute-start(f32[16,3072]{1,0:T(8,128)S(1)} %fusion), channel_id=1, source_target_pairs={{0,14},{1,15},{2,16},{3,17},{4,18},{5,19},{6,20},{7,21},{8,22},{9,... | collective-permute-start | bytes 589832
  620.9 58.9 %collective-permute-start.12 = (f32[16,3072]{1,0:T(8,128)S(1)}, f32[16,3072]{1,0:T(8,128)S(1)}, u32[]{:S(2)}, u32[]{:S(2)}) collective-permute-start(f32[16,3072]{1,0:T(8,128)S(1)} %fusion), channel_id=1, source_target_pairs={{0,13},{1,14},{2,15},{3,16},{4,17},{5,18},{6,19},{7,20},{8,21},{9,... | collective-permute-start | bytes 589832
  631.2 50.6 %collective-permute-start.11 = (f32[16,3072]{1,0:T(8,128)S(1)}, f32[16,3072]{1,0:T(8,128)S(1)}, u32[]{:S(2)}, u32[]{:S(2)}) collective-permute-start(f32[16,3072]{1,0:T(8,128)S(1)} %fusion), channel_id=1, source_target_pairs={{0,12},{1,13},{2,14},{3,15},{4,16},{5,17},{6,18},{7,19},{8,20},{9,... | collective-permute-start | bytes 589832
  646.0 38.4 %collective-permute-start.10 = (f32[16,3072]{1,0:T(8,128)S(1)}, f32[16,3072]{1,0:T(8,128)S(1)}, u32[]{:S(2)}, u32[]{:S(2)}) collective-permute-start(f32[16,3072]{1,0:T(8,128)S(1)} %fusion), channel_id=1, source_target_pairs={{0,11},{1,12},{2,13},{3,14},{4,15},{5,16},{6,17},{7,18},{8,19},{9,... | collective-permute-start | bytes 589832
  673.3 23.7 %collective-permute-start.9 = (f32[16,3072]{1,0:T(8,128)S(1)}, f32[16,3072]{1,0:T(8,128)S(1)}, u32[]{:S(2)}, u32[]{:S(2)}) collective-permute-start(f32[16,3072]{1,0:T(8,128)S(1)} %fusion), channel_id=1, source_target_pairs={{0,10},{1,11},{2,12},{3,13},{4,14},{5,15},{6,16},{7,17},{8,18},{9,... | collective-permute-start | bytes 589832
  674.6 29.1 %collective-permute-start.8 = (f32[16,3072]{1,0:T(8,128)S(1)}, f32[16,3072]{1,0:T(8,128)S(1)}, u32[]{:S(2)}, u32[]{:S(2)}) collective-permute-start(f32[16,3072]{1,0:T(8,128)S(1)} %fusion), channel_id=1, source_target_pairs={{0,9},{1,10},{2,11},{3,12},{4,13},{5,14},{6,15},{7,16},{8,17},{9,1... | collective-permute-start | bytes 589832
  679.9 25.8 %collective-permute-start.7 = (f32[16,3072]{1,0:T(8,128)S(1)}, f32[16,3072]{1,0:T(8,128)S(1)}, u32[]{:S(2)}, u32[]{:S(2)}) collective-permute-start(f32[16,3072]{1,0:T(8,128)S(1)} %fusion), channel_id=1, source_target_pairs={{0,8},{1,9},{2,10},{3,11},{4,12},{5,13},{6,14},{7,15},{8,16},{9,17... | collective-permute-start | bytes 589832
  681.8 28.5 %collective-permute-start.6 = (f32[16,3072]{1,0:T(8,128)S(1)}, f32[16,3072]{1,0:T(8,128)S(1)}, u32[]{:S(2)}, u32[]{:S(2)}) collective-permute-start(f32[16,3072]{1,0:T(8,128)S(1)} %fusion), channel_id=1, source_target_pairs={{0,7},{1,8},{2,9},{3,10},{4,11},{5,12},{6,13},{7,14},{8,15},{9,16}... | collective-permute-start | bytes 589832
  685.1 27.1 %collective-permute-start.5 = (f32[16,3072]{1,0:T(8,128)S(1)}, f32[16,3072]{1,0:T(8,128)S(1)}, u32[]{:S(2)}, u32[]{:S(2)}) collective-permute-start(f32[16,3072]{1,0:T(8,128)S(1)} %fusion), channel_id=1, source_target_pairs={{0,6},{1,7},{2,8},{3,9},{4,10},{5,11},{6,12},{7,13},{8,14},{9,15},... | collective-permute-start | bytes 589832
  697.0 25.4 %collective-permute-start.4 = (f32[16,3072]{1,0:T(8,128)S(1)}, f32[16,3072]{1,0:T(8,128)}, u32[]{:S(2)}, u32[]{:S(2)}) collective-permute-start(f32[16,3072]{1,0:T(8,128)S(1)} %fusion), channel_id=1, source_target_pairs={{0,5},{1,6},{2,7},{3,8},{4,9},{5,10},{6,11},{7,12},{8,13},{9,14},{... | collective-permute-start | bytes 589832
  703.7 18.6 %collective-permute-start.3 = (f32[16,3072]{1,0:T(8,128)S(1)}, f32[16,3072]{1,0:T(8,128)}, u32[]{:S(2)}, u32[]{:S(2)}) collective-permute-start(f32[16,3072]{1,0:T(8,128)S(1)} %fusion), channel_id=1, source_target_pairs={{0,4},{1,5},{2,6},{3,7},{4,8},{5,9},{6,10},{7,11},{8,12},{9,13},{1... | collective-permute-start | bytes 589832
  705.7 16.7 %collective-permute-start.2 = (f32[16,3072]{1,0:T(8,128)S(1)}, f32[16,3072]{1,0:T(8,128)}, u32[]{:S(2)}, u32[]{:S(2)}) collective-permute-start(f32[16,3072]{1,0:T(8,128)S(1)} %fusion), channel_id=1, source_target_pairs={{0,3},{1,4},{2,5},{3,6},{4,7},{5,8},{6,9},{7,10},{8,11},{9,12},{10... | collective-permute-start | bytes 589832
  710.3 12.1 %collective-permute-start.1 = (f32[16,3072]{1,0:T(8,128)S(1)}, f32[16,3072]{1,0:T(8,128)}, u32[]{:S(2)}, u32[]{:S(2)}) collective-permute-start(f32[16,3072]{1,0:T(8,128)S(1)} %fusion), channel_id=1, source_target_pairs={{0,2},{1,3},{2,4},{3,5},{4,6},{5,7},{6,8},{7,9},{8,10},{9,11},{10,... | collective-permute-start | bytes 589832
  712.9 9.5 %collective-permute-start = (f32[16,3072]{1,0:T(8,128)S(1)}, f32[16,3072]{1,0:T(8,128)}, u32[]{:S(2)}, u32[]{:S(2)}) collective-permute-start(f32[16,3072]{1,0:T(8,128)S(1)} %fusion), channel_id=1, source_target_pairs={{0,1},{1,2},{2,3},{3,4},{4,5},{5,6},{6,7},{7,8},{8,9},{9,10},{10,1... | collective-permute-start | bytes 589832
  722.3 86.6 %copy-start.52 = (f32[16,48]{1,0:T(8,128)S(1)}, f32[16,48]{1,0:T(8,128)}, u32[]{:S(2)}) copy-start(f32[16,48]{1,0:T(8,128)} %copy-done.51) | copy-start | bytes 9220
  722.3 86.6 %copy-start.60 = (f32[16,48]{1,0:T(8,128)S(1)}, f32[16,48]{1,0:T(8,128)}, u32[]{:S(2)}) copy-start(f32[16,48]{1,0:T(8,128)} %copy-done.59) | copy-start | bytes 9220
  722.3 86.6 %copy-start.62 = (f32[1536]{0:T(1024)S(1)}, f32[1536]{0:T(1024)}, u32[]{:S(2)}) copy-start(f32[1536]{0:T(1024)} %param.10) | copy-start | bytes 18436
  722.3 187.8 %all-gather.6.cloned.1.call-start = ((), (), s32[]{:S(2)}) async-start(), calls=%async_computation.2 | async-start | bytes 3342336 | tf_op jit(solution)/shard_map/all_gather | solution.py:111
  (46 other events, 831.2 us)
Sparse Core Ops, SparseCore 0:
  9.7 57.9 all-gather.3
  722.4 139.3 all-reduce.6
  864.2 45.8 all-gather.5
where the time goes:
time: 927 us; the launch traced here: 924 us
  blocking collectives  424 us (46%)
  other arithmetic  145 us (16%)
  starting transfers between devices  136 us (15%)
  local copies, waits for them, and re-layouts  128 us (14%)
  waiting for transfers between devices  38.2 us (4%)
  matrix products  35.9 us (4%)
  between operations  16.2 us (2%)
    unnamed x1, blocking collectives  360 us
    unnamed x32, starting transfers between devices  136 us
    unnamed x153, local copies, waits for them, and re-layouts  92.8 us
    reduce_sum x4, other arithmetic, block_pass(): kernel_terms.append(jnp.sum(grad_conv * window * same_seg, axis=(0, 1)))  88.1 us
    psum x1, blocking collectives, local(): kernel_total, gain_total = lax.psum((kernel_part, gain_part), ('dp', 'red'))  63.9 us
    another operation x2, other arithmetic  35.5 us
    all_gather x1, waiting for transfers between devices, local(): weights = lax.all_gather(w_in, 'red', axis=0, tiled=True)  23.9 us
  transfers between devices with their start and end apart: 35, of which 3 were waited for; matrix products, arithmetic and copies ran while one was open for 20% of the time, Pallas kernels for 0%

commit v1 on v0

--- a/solution.py
+++ b/solution.py
@@ -109,7 +109,7 @@
         tiled=True,
     )
     grad_weights = lax.all_gather(owned_rows, "dp", axis=0, tiled=True)
-    kernel_total, gain_total = lax.psum((kernel_part, gain_part), ("dp", "red"))
+    kernel_total, gain_total = lax.psum(lax.psum((kernel_part, gain_part), "dp"), "red")
     return (
         module_output,
         frame_gradient,

time: 927 us -> 995 us (1.073)
  waiting for transfers between devices: 38.2 us -> 106 us
  blocking collectives: 424 us -> 413 us
    psum x1 -> x2, waiting for transfers between devices: 0.01 us -> 80 us  [the longest x1 80 us: local(): lax.psum((kernel_part, gain_part), 'dp')]
    all_gather x1, waiting for transfers between devices: 12.9 us -> 0.01 us  [local(): grad_weights = lax.all_gather(owned_rows, 'dp', axis=0, tiled=True)]
    psum x1 -> x2, blocking collectives: 63.9 us -> 53 us  [the longest x1 31.9 us: local(): lax.psum((kernel_part, gain_part), 'dp')]
    unnamed x153 -> x177, local copies, waits for them, and re-layouts: 92.8 us -> 93.3 us
  transfers between devices with their start and end apart: 35 -> 36, of which waited for: 3 -> 3; matrix products, arithmetic and copies ran while one was open for 20% -> 20% of each run, Pallas kernels for 0% -> 0%
where the time goes in v1:
time: 995 us; the launch traced here: 991 us
  blocking collectives  413 us (42%)
  other arithmetic  147 us (15%)
  starting transfers between devices  139 us (14%)
  local copies, waits for them, and re-layouts  134 us (13%)
  waiting for transfers between devices  106 us (11%)
  matrix products  35.9 us (4%)
  between operations  16.4 us (2%)
    unnamed x1, blocking collectives  360 us
    unnamed x32, starting transfers between devices  139 us
    unnamed x177, local copies, waits for them, and re-layouts  93.3 us
    reduce_sum x4, other arithmetic, block_pass(): kernel_terms.append(jnp.sum(grad_conv * window * same_seg, axis=(0, 1)))  89.1 us
    psum x1, waiting for transfers between devices, local(): lax.psum((kernel_part, gain_part), 'dp')  80 us
    another operation x2, other arithmetic  35.5 us
    psum x1, blocking collectives, local(): lax.psum((kernel_part, gain_part), 'dp')  31.9 us
    all_gather x1, waiting for transfers between devices, local(): weights = lax.all_gather(w_in, 'red', axis=0, tiled=True)  23.9 us
  transfers between devices with their start and end apart: 36, of which 3 were waited for; matrix products, arithmetic and copies ran while one was open for 20% of the time, Pallas kernels for 0%

profile of v1, /device:TPU:1, one launch (start us, length us, event | category | flops | bytes accessed | tf_op | source)
XLA Modules:
  0.0 990.9 jit_solution(7184912724434476179)
XLA Ops:
  8.8 2.1 convert_reduce_fusion
  12.2 2.2 fusion.11
  14.4 8.3 copy.13
  22.7 10.7 %reshape_reshape.3 = bf16[768,8,16,12]{0,3,2,1:T(8,128)(2,1)} reshape(bf16[16,48,1536]{1,0,2:T(8,128)(2,1)} %copy.13) | data formatting | bytes 4718592 | tf_op jit(solution)/shard_map/reshape;reshape | solution.py:101
  33.4 4.0 copy.14
  37.4 5.2 reshape.139
  43.8 23.9 %all-gather.4.cloned.1.call-done = bf16[1536,3072]{1,0:T(8,128)(2,1)} async-done(((bf16[192,3072]{1,0:T(8,128)(2,1)}), bf16[1536,3072]{1,0:T(8,128)(2,1)}) %all-gather.4.cloned.1.call-update) | async-done | bytes 9437200 | tf_op jit(solution)/shard_map/all_gather | solution.py:88
  67.7 10.8 %fusion.3 = f32[16,48,3072]{2,1,0:T(8,128)S(1)} fusion(bf16[16,48,1536]{2,1,0:T(8,128)(2,1)} %fusion.11, bf16[1536,3072]{1,0:T(8,128)(2,1)} %all-gather.4.cloned.1.call-done), kind=kOutput, calls=%fused_computation.62 | convolution fusion | flops 7247757312 | bytes 21233664 | tf_op jit(solution)/shard_map/dot_general | solution.py:23
  78.6 1.3 multiply_multiply_fusion.1
  79.9 2.7 copy-done.2
  82.6 49.2 %multiply_reduce_fusion = (f32[1536]{0:T(1024)}, f32[1536]{0:T(1024)}, f32[1536]{0:T(1024)}, f32[1536]{0:T(1024)}, f32[1536]{0:T(1024)}, /*index=5*/f32[1536]{0:...) fusion(f32[16,48,1536]{2,1,0:T(8,128)S(1)} %multiply_multiply_f, ...), kind=kLoop, calls=%fused_computation.186 | loop fusion | flops 150981120 | bytes 16856064 | tf_op jit(solution)/shard_map/reduce_sum | solution.py:50
  132.0 28.6 %multiply_convert_fusion.1 = (bf16[16,48,1536]{2,1,0:T(8,128)(2,1)S(1)}, f32[16,48,1536]{2,1,0:T(8,128)}) fusion(f32[16,48,3072]{2,1,0:T(8,128)} %copy-done.2, f32[16,48]{1,0:T(8,128)S(1)} %get-tuple-element.106, f32[16,48]{1,0:T(8,128)S(1)} %get-tuple-element.76, f32[1536]{0:T(1024)} %copy-done.68, f32[16,48]{1,0:T(8,128)S(1)} %get-tuple-element.77, ...), kind=kLoop, calls=%fused_computation.218 | loop fusion | flops 114425856 | bytes 16800768 | tf_op jit(solution)/shard_map/convert.4
  160.6 6.9 multiply_convert_fusion
  167.5 1.4 copy-done.6
  168.9 10.8 %fusion.119 = f32[1536,3072]{1,0:T(8,128)} fusion(bf16[768,1536]{0,1:T(8,128)(2,1)S(1)} %copy-done.7, bf16[768,1536]{1,0:T(8,128)(2,1)S(1)} %bitcast.26, bf16[768,1536]{1,0:T(8,128)(2,1)S(1)} %bitcast.25), kind=kOutput, calls=%fused_computation.182 | convolution fusion | flops 7257194496 | bytes 25952256 | tf_op jit(solution)/shard_map/dot_general | solution.py:104
  179.8 359.8 %fusion = f32[16,3072]{1,0:T(8,128)S(1)} fusion(f32[1536,3072]{1,0:T(8,128)} %fusion.119), kind=kCustom, calls=%all-reduce-scatter | all-reduce-scatter fusion | flops 6291457 | bytes 19070976
  539.7 1.3 collective-permute-start.30
  541.1 1.6 collective-permute-start.31
  542.6 1.3 collective-permute-start.29
  543.9 1.3 collective-permute-start.28
  545.2 1.3 collective-permute-start.27
  546.6 1.3 collective-permute-start.26
  547.9 1.3 collective-permute-start.25
  549.2 1.3 collective-permute-start.24
  550.5 1.3 collective-permute-start.23
  551.9 0.9 collective-permute-done.27
  552.7 15.0 %collective-permute-start.22 = (f32[16,3072]{1,0:T(8,128)S(1)}, f32[16,3072]{1,0:T(8,128)S(1)}, u32[]{:S(2)}, u32[]{:S(2)}) collective-permute-start(f32[16,3072]{1,0:T(8,128)S(1)} %fusion), channel_id=1, source_target_pairs={{0,23},{1,24},{2,25},{3,26},{4,27},{5,28},{6,29},{7,30},{8,31},{9,... | collective-permute-start | bytes 589832
  567.7 6.4 collective-permute-start.21
  574.1 5.7 collective-permute-start.20
  579.8 7.7 collective-permute-start.19
  587.6 1.3 collective-permute-start.18
  588.9 6.6 collective-permute-start.17
  595.6 1.3 collective-permute-start.16
  596.9 4.3 collective-permute-start.15
  601.2 5.9 collective-permute-start.14
  607.1 12.3 %collective-permute-start.13 = (f32[16,3072]{1,0:T(8,128)S(1)}, f32[16,3072]{1,0:T(8,128)S(1)}, u32[]{:S(2)}, u32[]{:S(2)}) collective-permute-start(f32[16,3072]{1,0:T(8,128)S(1)} %fusion), channel_id=1, source_target_pairs={{0,14},{1,15},{2,16},{3,17},{4,18},{5,19},{6,20},{7,21},{8,22},{9,... | collective-permute-start | bytes 589832
  619.4 10.3 %collective-permute-start.12 = (f32[16,3072]{1,0:T(8,128)S(1)}, f32[16,3072]{1,0:T(8,128)S(1)}, u32[]{:S(2)}, u32[]{:S(2)}) collective-permute-start(f32[16,3072]{1,0:T(8,128)S(1)} %fusion), channel_id=1, source_target_pairs={{0,13},{1,14},{2,15},{3,16},{4,17},{5,18},{6,19},{7,20},{8,21},{9,... | collective-permute-start | bytes 589832
  629.8 14.7 %collective-permute-start.11 = (f32[16,3072]{1,0:T(8,128)S(1)}, f32[16,3072]{1,0:T(8,128)S(1)}, u32[]{:S(2)}, u32[]{:S(2)}) collective-permute-start(f32[16,3072]{1,0:T(8,128)S(1)} %fusion), channel_id=1, source_target_pairs={{0,12},{1,13},{2,14},{3,15},{4,16},{5,17},{6,18},{7,19},{8,20},{9,... | collective-permute-start | bytes 589832
  645.3 1.3 collective-permute-start.10
  646.7 26.1 %multiply_reduce_fusion.9 = (f32[1536]{0:T(1024)S(1)}, f32[1536]{0:T(1024)S(1)}, f32[1536]{0:T(1024)S(1)}, f32[1536]{0:T(1024)S(1)}, f32[1536]{0:T(1024)S(1)}, /...) fusion(f32[16,48,1536]{2,1,0:T(8,128)} %copy-done.1, f32[16,48,1536]{2,1,0:T(8,128)} %copy-done, ...), kind=kLoop, calls=%fused_computation.195 | loop fusion | flops 30657024 | bytes 9517056 | tf_op jit(solution)/shard_map/reduce_sum | solution.py:50
  672.8 1.4 collective-permute-start.9
  674.3 5.2 collective-permute-start.8
  679.5 1.9 collective-permute-start.7
  681.5 2.5 collective-permute-start.6
  684.7 3.5 collective-permute-start.5
  688.2 9.8 multiply_reduce_fusion.18
  698.2 5.9 collective-permute-start.4
  704.1 2.0 collective-permute-start.3
  706.1 6.9 collective-permute-start.2
  713.1 2.2 collective-permute-start.1
  716.0 2.7 collective-permute-start
  718.8 3.9 multiply_reduce_fusion.27
  727.3 4.2 stack.127
  731.6 1.4 reduce_sum.337
  733.7 80.0 %all-reduce.8.cloned.1.call-done = f32[31,1536]{1,0:T(8,128)} async-done(((f32[31,1536]{1,0:T(8,128)}), f32[31,1536]{1,0:T(8,128)}) %all-reduce.8.cloned.1.call-update) | async-done | bytes 190480 | tf_op jit(solution)/shard_map/psum | solution.py:112
  813.8 84.6 %concatenate.17 = f32[524,3072]{1,0:T(8,128)} concatenate(f32[12,3072]{1,0:T(8,128)S(1)} %collective-permute-done.31, f32[16,3072]{1,0:T(8,128)S(1)} %collective-permute-done.30, f32[16,3072]{1,0:T(8,128)S(1)} %collective-permute-done.29, f32[16,3072]{1,0:T(8,128)S(1)} %copy-done.9, f32[16,3072]{1,0:T(8,128)} %copy-done.10, f32[16,3072]{1,0:T(8,128)} %copy-done.11, ...), dimensions={0} | concatenate | bytes 12877824
  898.4 1.7 dynamic-slice_bitcast_fusion
  900.1 14.3 %fusion.18 = (f32[1536]{0:T(1024)S(1)}, f32[16,48]{1,0:T(8,128)S(1)}, f32[16,48]{1,0:T(8,128)S(1)}, f32[16,48,1536]{2,1,0:T(8,128)}) fusion(bf16[16,48,1536]{2,1,0:T(8,128)(2,1)S(1)} %copy-done.3, f32[16,48]{1,0:T(8,128)S(1)} %copy-done.71, f32[16,48]{1,0:T(8,128)S(1)} %copy-done.63, f32[1536]{0:T(1024)S(1)} %copy-done.73, ...), kind=kOutput, calls=%fused_computation.80 | convolution fusion | flops 7267808256 | bytes 21258240 | tf_op jit(solution)/shard_map/dot_general | solution.py:67
  914.4 31.9 %psum.30 = f32[1536]{0:T(1024)S(1)} all-reduce(f32[1536]{0:T(1024)S(1)} %get-tuple-element.36), channel_id=1, replica_groups=mesh['dp'=16,'red'=8] {'dp'}, use_global_device_ids=true, to_apply=%region_40.41 | all-reduce | flops 1536 | bytes 12288 | tf_op jit(solution)/shard_map/psum | solution.py:112
  946.2 21.1 %psum.31 = f32[1536]{0:T(1024)S(1)} all-reduce(f32[1536]{0:T(1024)S(1)} %psum.30), channel_id=1, replica_groups=mesh['dp'=16,'red'=8] {'red'}, use_global_device_ids=true, to_apply=%region_41.42 | all-reduce | flops 1536 | bytes 12288 | tf_op jit(solution)/shard_map/psum | solution.py:112
  968.0 7.8 fusion.17
  975.8 1.6 broadcast_multiply_fusion.1
  977.4 3.9 broadcast_multiply_fusion
  981.3 3.0 reshape.143
  (261 shorter events, 11.4 us)
Async XLA Ops:
  7.2 60.5 %all-gather.4.cloned.1.call-start = ((), (), s32[]{:S(2)}) async-start(), calls=%async_computation | async-start | bytes 10616832 | tf_op jit(solution)/shard_map/all_gather | solution.py:88
  7.9 805.7 %all-reduce.8.cloned.1.call-start = ((), (), s32[]{:S(2)}) async-start(), calls=%async_computation.1 | async-start | bytes 393216 | tf_op jit(solution)/shard_map/psum | solution.py:112
  43.5 88.4 %copy-start.46 = (f32[16,48]{1,0:T(8,128)}, f32[16,48]{1,0:T(8,128)S(1)}, u32[]{:S(2)}) copy-start(f32[16,48]{1,0:T(8,128)S(1)} %get-tuple-element.89) | copy-start | bytes 9220
  43.5 88.4 %copy-start.48 = (f32[16,48]{1,0:T(8,128)}, f32[16,48]{1,0:T(8,128)S(1)}, u32[]{:S(2)}) copy-start(f32[16,48]{1,0:T(8,128)S(1)} %get-tuple-element.90) | copy-start | bytes 9220
  43.5 88.4 %copy-start.50 = (f32[16,48]{1,0:T(8,128)}, f32[16,48]{1,0:T(8,128)S(1)}, u32[]{:S(2)}) copy-start(f32[16,48]{1,0:T(8,128)S(1)} %get-tuple-element.91) | copy-start | bytes 9220
  43.5 88.4 %copy-start.52 = (f32[16,48]{1,0:T(8,128)}, f32[16,48]{1,0:T(8,128)S(1)}, u32[]{:S(2)}) copy-start(f32[16,48]{1,0:T(8,128)S(1)} %get-tuple-element.92) | copy-start | bytes 9220
  43.5 88.4 %copy-start.54 = (f32[16,48]{1,0:T(8,128)}, f32[16,48]{1,0:T(8,128)S(1)}, u32[]{:S(2)}) copy-start(f32[16,48]{1,0:T(8,128)S(1)} %get-tuple-element.93) | copy-start | bytes 9220
  43.6 88.3 %copy-start.56 = (f32[16,48]{1,0:T(8,128)}, f32[16,48]{1,0:T(8,128)S(1)}, u32[]{:S(2)}) copy-start(f32[16,48]{1,0:T(8,128)S(1)} %get-tuple-element.94) | copy-start | bytes 9220
  43.6 88.3 %copy-start.58 = (f32[16,48]{1,0:T(8,128)}, f32[16,48]{1,0:T(8,128)S(1)}, u32[]{:S(2)}) copy-start(f32[16,48]{1,0:T(8,128)S(1)} %get-tuple-element.95) | copy-start | bytes 9220
  43.6 88.3 %copy-start.60 = (f32[16,48]{1,0:T(8,128)}, f32[16,48]{1,0:T(8,128)S(1)}, u32[]{:S(2)}) copy-start(f32[16,48]{1,0:T(8,128)S(1)} %get-tuple-element.96) | copy-start | bytes 9220
  43.7 88.2 %copy-start.34 = (f32[16,48]{1,0:T(8,128)}, f32[16,48]{1,0:T(8,128)S(1)}, u32[]{:S(2)}) copy-start(f32[16,48]{1,0:T(8,128)S(1)} %get-tuple-element.79) | copy-start | bytes 9220
  179.7 466.8 %copy-start.47 = (f32[16,48]{1,0:T(8,128)S(1)}, f32[16,48]{1,0:T(8,128)}, u32[]{:S(2)}) copy-start(f32[16,48]{1,0:T(8,128)} %copy-done.46) | copy-start | bytes 9220
  179.7 466.8 %copy-start.49 = (f32[16,48]{1,0:T(8,128)S(1)}, f32[16,48]{1,0:T(8,128)}, u32[]{:S(2)}) copy-start(f32[16,48]{1,0:T(8,128)} %copy-done.48) | copy-start | bytes 9220
  179.8 466.9 %copy-start.51 = (f32[16,48]{1,0:T(8,128)S(1)}, f32[16,48]{1,0:T(8,128)}, u32[]{:S(2)}) copy-start(f32[16,48]{1,0:T(8,128)} %copy-done.50) | copy-start | bytes 9220
  179.8 466.9 %copy-start.53 = (f32[16,48]{1,0:T(8,128)S(1)}, f32[16,48]{1,0:T(8,128)}, u32[]{:S(2)}) copy-start(f32[16,48]{1,0:T(8,128)} %copy-done.52) | copy-start | bytes 9220
  179.8 466.9 %copy-start.55 = (f32[16,48]{1,0:T(8,128)S(1)}, f32[16,48]{1,0:T(8,128)}, u32[]{:S(2)}) copy-start(f32[16,48]{1,0:T(8,128)} %copy-done.54) | copy-start | bytes 9220
  179.8 466.9 %copy-start.57 = (f32[16,48]{1,0:T(8,128)S(1)}, f32[16,48]{1,0:T(8,128)}, u32[]{:S(2)}) copy-start(f32[16,48]{1,0:T(8,128)} %copy-done.56) | copy-start | bytes 9220
  179.8 466.9 %copy-start.59 = (f32[16,48]{1,0:T(8,128)S(1)}, f32[16,48]{1,0:T(8,128)}, u32[]{:S(2)}) copy-start(f32[16,48]{1,0:T(8,128)} %copy-done.58) | copy-start | bytes 9220
  179.8 466.9 %copy-start.61 = (f32[16,48]{1,0:T(8,128)S(1)}, f32[16,48]{1,0:T(8,128)}, u32[]{:S(2)}) copy-start(f32[16,48]{1,0:T(8,128)} %copy-done.60) | copy-start | bytes 9220
  539.7 8.2 collective-permute-start.30
  541.0 147.2 %slice-start = ((s8[4718592]{0:T(1024)(128)(4,1)}), s8[4194304]{0:T(1024)(128)(4,1)S(1)}, s32[]{:S(2)}) async-start(s8[4718592]{0:T(1024)(128)(4,1)} %bitcast.20), calls=%async_computation.4 | async-start | bytes 8388608
  541.0 147.2 %slice-start.1 = ((s8[4718592]{0:T(1024)(128)(4,1)}), s8[524288]{0:T(1024)(128)(4,1)S(1)}, s32[]{:S(2)}) async-start(s8[4718592]{0:T(1024)(128)(4,1)} %bitcast.20), calls=%async_computation.5 | async-start | bytes 1048576
  541.0 147.2 %copy-start.37 = (f32[16,48]{1,0:T(8,128)S(1)}, f32[16,48]{1,0:T(8,128)}, u32[]{:S(2)}) copy-start(f32[16,48]{1,0:T(8,128)} %copy-done.36) | copy-start | bytes 9220
  541.0 147.2 %copy-start.39 = (f32[16,48]{1,0:T(8,128)S(1)}, f32[16,48]{1,0:T(8,128)}, u32[]{:S(2)}) copy-start(f32[16,48]{1,0:T(8,128)} %copy-done.38) | copy-start | bytes 9220
  541.0 147.2 %copy-start.41 = (f32[16,48]{1,0:T(8,128)S(1)}, f32[16,48]{1,0:T(8,128)}, u32[]{:S(2)}) copy-start(f32[16,48]{1,0:T(8,128)} %copy-done.40) | copy-start | bytes 9220
  541.0 147.2 %copy-start.43 = (f32[16,48]{1,0:T(8,128)S(1)}, f32[16,48]{1,0:T(8,128)}, u32[]{:S(2)}) copy-start(f32[16,48]{1,0:T(8,128)} %copy-done.42) | copy-start | bytes 9220
  541.0 147.2 %copy-start.45 = (f32[16,48]{1,0:T(8,128)S(1)}, f32[16,48]{1,0:T(8,128)}, u32[]{:S(2)}) copy-start(f32[16,48]{1,0:T(8,128)} %copy-done.44) | copy-start | bytes 9220
  541.1 5.5 collective-permute-start.31
  542.6 6.6 collective-permute-start.29
  543.9 6.6 collective-permute-start.28
  545.2 7.5 collective-permute-start.27
  546.6 21.1 %collective-permute-start.26 = (f32[16,3072]{1,0:T(8,128)S(1)}, f32[16,3072]{1,0:T(8,128)S(1)}, u32[]{:S(2)}, u32[]{:S(2)}) collective-permute-start(f32[16,3072]{1,0:T(8,128)S(1)} %fusion), channel_id=1, source_target_pairs={{0,27},{1,28},{2,29},{3,30},{4,31},{5,32},{6,33},{7,34},{8,35},{9,... | collective-permute-start | bytes 589832
  547.9 26.2 %collective-permute-start.25 = (f32[16,3072]{1,0:T(8,128)S(1)}, f32[16,3072]{1,0:T(8,128)S(1)}, u32[]{:S(2)}, u32[]{:S(2)}) collective-permute-start(f32[16,3072]{1,0:T(8,128)S(1)} %fusion), channel_id=1, source_target_pairs={{0,26},{1,27},{2,28},{3,29},{4,30},{5,31},{6,32},{7,33},{8,34},{9,... | collective-permute-start | bytes 589832
  549.2 30.6 %collective-permute-start.24 = (f32[16,3072]{1,0:T(8,128)S(1)}, f32[16,3072]{1,0:T(8,128)S(1)}, u32[]{:S(2)}, u32[]{:S(2)}) collective-permute-start(f32[16,3072]{1,0:T(8,128)S(1)} %fusion), channel_id=1, source_target_pairs={{0,25},{1,26},{2,27},{3,28},{4,29},{5,30},{6,31},{7,32},{8,33},{9,... | collective-permute-start | bytes 589832
  550.5 94.0 %copy-start.8 = (f32[16,3072]{1,0:T(8,128)}, f32[16,3072]{1,0:T(8,128)S(1)}, u32[]{:S(2)}) copy-start(f32[16,3072]{1,0:T(8,128)S(1)} %collective-permute-done.28) | copy-start | bytes 589828
  550.5 37.0 %collective-permute-start.23 = (f32[16,3072]{1,0:T(8,128)S(1)}, f32[16,3072]{1,0:T(8,128)S(1)}, u32[]{:S(2)}, u32[]{:S(2)}) collective-permute-start(f32[16,3072]{1,0:T(8,128)S(1)} %fusion), channel_id=1, source_target_pairs={{0,24},{1,25},{2,26},{3,27},{4,28},{5,29},{6,30},{7,31},{8,32},{9,... | collective-permute-start | bytes 589832
  552.7 91.8 %copy-start.10 = (f32[16,3072]{1,0:T(8,128)}, f32[16,3072]{1,0:T(8,128)S(1)}, u32[]{:S(2)}) copy-start(f32[16,3072]{1,0:T(8,128)S(1)} %collective-permute-done.27) | copy-start | bytes 589828
  552.7 36.1 %collective-permute-start.22 = (f32[16,3072]{1,0:T(8,128)S(1)}, f32[16,3072]{1,0:T(8,128)S(1)}, u32[]{:S(2)}, u32[]{:S(2)}) collective-permute-start(f32[16,3072]{1,0:T(8,128)S(1)} %fusion), channel_id=1, source_target_pairs={{0,23},{1,24},{2,25},{3,26},{4,27},{5,28},{6,29},{7,30},{8,31},{9,... | collective-permute-start | bytes 589832
  567.7 105.0 %copy-start.11 = (f32[16,3072]{1,0:T(8,128)}, f32[16,3072]{1,0:T(8,128)S(1)}, u32[]{:S(2)}) copy-start(f32[16,3072]{1,0:T(8,128)S(1)} %collective-permute-done.26) | copy-start | bytes 589828
  567.7 27.8 %collective-permute-start.21 = (f32[16,3072]{1,0:T(8,128)S(1)}, f32[16,3072]{1,0:T(8,128)S(1)}, u32[]{:S(2)}, u32[]{:S(2)}) collective-permute-start(f32[16,3072]{1,0:T(8,128)S(1)} %fusion), channel_id=1, source_target_pairs={{0,22},{1,23},{2,24},{3,25},{4,26},{5,27},{6,28},{7,29},{8,30},{9,... | collective-permute-start | bytes 589832
  574.1 22.8 %collective-permute-start.20 = (f32[16,3072]{1,0:T(8,128)S(1)}, f32[16,3072]{1,0:T(8,128)S(1)}, u32[]{:S(2)}, u32[]{:S(2)}) collective-permute-start(f32[16,3072]{1,0:T(8,128)S(1)} %fusion), channel_id=1, source_target_pairs={{0,21},{1,22},{2,23},{3,24},{4,25},{5,26},{6,27},{7,28},{8,29},{9,... | collective-permute-start | bytes 589832
  579.8 21.4 %collective-permute-start.19 = (f32[16,3072]{1,0:T(8,128)S(1)}, f32[16,3072]{1,0:T(8,128)S(1)}, u32[]{:S(2)}, u32[]{:S(2)}) collective-permute-start(f32[16,3072]{1,0:T(8,128)S(1)} %fusion), channel_id=1, source_target_pairs={{0,20},{1,21},{2,22},{3,23},{4,24},{5,25},{6,26},{7,27},{8,28},{9,... | collective-permute-start | bytes 589832
  587.6 19.6 %collective-permute-start.18 = (f32[16,3072]{1,0:T(8,128)S(1)}, f32[16,3072]{1,0:T(8,128)S(1)}, u32[]{:S(2)}, u32[]{:S(2)}) collective-permute-start(f32[16,3072]{1,0:T(8,128)S(1)} %fusion), channel_id=1, source_target_pairs={{0,19},{1,20},{2,21},{3,22},{4,23},{5,24},{6,25},{7,26},{8,27},{9,... | collective-permute-start | bytes 589832
  588.9 30.5 %collective-permute-start.17 = (f32[16,3072]{1,0:T(8,128)S(1)}, f32[16,3072]{1,0:T(8,128)S(1)}, u32[]{:S(2)}, u32[]{:S(2)}) collective-permute-start(f32[16,3072]{1,0:T(8,128)S(1)} %fusion), channel_id=1, source_target_pairs={{0,18},{1,19},{2,20},{3,21},{4,22},{5,23},{6,24},{7,25},{8,26},{9,... | collective-permute-start | bytes 589832
  595.6 34.2 %collective-permute-start.16 = (f32[16,3072]{1,0:T(8,128)S(1)}, f32[16,3072]{1,0:T(8,128)S(1)}, u32[]{:S(2)}, u32[]{:S(2)}) collective-permute-start(f32[16,3072]{1,0:T(8,128)S(1)} %fusion), channel_id=1, source_target_pairs={{0,17},{1,18},{2,19},{3,20},{4,21},{5,22},{6,23},{7,24},{8,25},{9,... | collective-permute-start | bytes 589832
  596.9 47.6 %collective-permute-start.15 = (f32[16,3072]{1,0:T(8,128)S(1)}, f32[16,3072]{1,0:T(8,128)S(1)}, u32[]{:S(2)}, u32[]{:S(2)}) collective-permute-start(f32[16,3072]{1,0:T(8,128)S(1)} %fusion), channel_id=1, source_target_pairs={{0,16},{1,17},{2,18},{3,19},{4,20},{5,21},{6,22},{7,23},{8,24},{9,... | collective-permute-start | bytes 589832
  601.2 71.5 %collective-permute-start.14 = (f32[16,3072]{1,0:T(8,128)S(1)}, f32[16,3072]{1,0:T(8,128)S(1)}, u32[]{:S(2)}, u32[]{:S(2)}) collective-permute-start(f32[16,3072]{1,0:T(8,128)S(1)} %fusion), channel_id=1, source_target_pairs={{0,15},{1,16},{2,17},{3,18},{4,19},{5,20},{6,21},{7,22},{8,23},{9,... | collective-permute-start | bytes 589832
  607.1 67.1 %collective-permute-start.13 = (f32[16,3072]{1,0:T(8,128)S(1)}, f32[16,3072]{1,0:T(8,128)S(1)}, u32[]{:S(2)}, u32[]{:S(2)}) collective-permute-start(f32[16,3072]{1,0:T(8,128)S(1)} %fusion), channel_id=1, source_target_pairs={{0,14},{1,15},{2,16},{3,17},{4,18},{5,19},{6,20},{7,21},{8,22},{9,... | collective-permute-start | bytes 589832
  619.4 60.1 %collective-permute-start.12 = (f32[16,3072]{1,0:T(8,128)S(1)}, f32[16,3072]{1,0:T(8,128)S(1)}, u32[]{:S(2)}, u32[]{:S(2)}) collective-permute-start(f32[16,3072]{1,0:T(8,128)S(1)} %fusion), channel_id=1, source_target_pairs={{0,13},{1,14},{2,15},{3,16},{4,17},{5,18},{6,19},{7,20},{8,21},{9,... | collective-permute-start | bytes 589832
  629.8 51.7 %collective-permute-start.11 = (f32[16,3072]{1,0:T(8,128)S(1)}, f32[16,3072]{1,0:T(8,128)S(1)}, u32[]{:S(2)}, u32[]{:S(2)}) collective-permute-start(f32[16,3072]{1,0:T(8,128)S(1)} %fusion), channel_id=1, source_target_pairs={{0,12},{1,13},{2,14},{3,15},{4,16},{5,17},{6,18},{7,19},{8,20},{9,... | collective-permute-start | bytes 589832
  645.3 38.7 %collective-permute-start.10 = (f32[16,3072]{1,0:T(8,128)S(1)}, f32[16,3072]{1,0:T(8,128)S(1)}, u32[]{:S(2)}, u32[]{:S(2)}) collective-permute-start(f32[16,3072]{1,0:T(8,128)S(1)} %fusion), channel_id=1, source_target_pairs={{0,11},{1,12},{2,13},{3,14},{4,15},{5,16},{6,17},{7,18},{8,19},{9,... | collective-permute-start | bytes 589832
  672.8 25.4 %collective-permute-start.9 = (f32[16,3072]{1,0:T(8,128)S(1)}, f32[16,3072]{1,0:T(8,128)S(1)}, u32[]{:S(2)}, u32[]{:S(2)}) collective-permute-start(f32[16,3072]{1,0:T(8,128)S(1)} %fusion), channel_id=1, source_target_pairs={{0,10},{1,11},{2,12},{3,13},{4,14},{5,15},{6,16},{7,17},{8,18},{9,... | collective-permute-start | bytes 589832
  674.3 29.9 %collective-permute-start.8 = (f32[16,3072]{1,0:T(8,128)S(1)}, f32[16,3072]{1,0:T(8,128)S(1)}, u32[]{:S(2)}, u32[]{:S(2)}) collective-permute-start(f32[16,3072]{1,0:T(8,128)S(1)} %fusion), channel_id=1, source_target_pairs={{0,9},{1,10},{2,11},{3,12},{4,13},{5,14},{6,15},{7,16},{8,17},{9,1... | collective-permute-start | bytes 589832
  679.5 26.6 %collective-permute-start.7 = (f32[16,3072]{1,0:T(8,128)S(1)}, f32[16,3072]{1,0:T(8,128)S(1)}, u32[]{:S(2)}, u32[]{:S(2)}) collective-permute-start(f32[16,3072]{1,0:T(8,128)S(1)} %fusion), channel_id=1, source_target_pairs={{0,8},{1,9},{2,10},{3,11},{4,12},{5,13},{6,14},{7,15},{8,16},{9,17... | collective-permute-start | bytes 589832
  681.5 31.6 %collective-permute-start.6 = (f32[16,3072]{1,0:T(8,128)S(1)}, f32[16,3072]{1,0:T(8,128)S(1)}, u32[]{:S(2)}, u32[]{:S(2)}) collective-permute-start(f32[16,3072]{1,0:T(8,128)S(1)} %fusion), channel_id=1, source_target_pairs={{0,7},{1,8},{2,9},{3,10},{4,11},{5,12},{6,13},{7,14},{8,15},{9,16}... | collective-permute-start | bytes 589832
  684.7 30.6 %collective-permute-start.5 = (f32[16,3072]{1,0:T(8,128)S(1)}, f32[16,3072]{1,0:T(8,128)S(1)}, u32[]{:S(2)}, u32[]{:S(2)}) collective-permute-start(f32[16,3072]{1,0:T(8,128)S(1)} %fusion), channel_id=1, source_target_pairs={{0,6},{1,7},{2,8},{3,9},{4,10},{5,11},{6,12},{7,13},{8,14},{9,15},... | collective-permute-start | bytes 589832
  698.2 115.6 %copy-start.9 = (f32[16,3072]{1,0:T(8,128)S(1)}, f32[16,3072]{1,0:T(8,128)}, u32[]{:S(2)}) copy-start(f32[16,3072]{1,0:T(8,128)} %copy-done.8) | copy-start | bytes 589828
  698.2 115.5 %collective-permute-start.4 = (f32[16,3072]{1,0:T(8,128)S(1)}, f32[16,3072]{1,0:T(8,128)}, u32[]{:S(2)}, u32[]{:S(2)}) collective-permute-start(f32[16,3072]{1,0:T(8,128)S(1)} %fusion), channel_id=1, source_target_pairs={{0,5},{1,6},{2,7},{3,8},{4,9},{5,10},{6,11},{7,12},{8,13},{9,14},{... | collective-permute-start | bytes 589832
  704.1 109.6 %collective-permute-start.3 = (f32[16,3072]{1,0:T(8,128)S(1)}, f32[16,3072]{1,0:T(8,128)}, u32[]{:S(2)}, u32[]{:S(2)}) collective-permute-start(f32[16,3072]{1,0:T(8,128)S(1)} %fusion), channel_id=1, source_target_pairs={{0,4},{1,5},{2,6},{3,7},{4,8},{5,9},{6,10},{7,11},{8,12},{9,13},{1... | collective-permute-start | bytes 589832
  706.1 107.6 %collective-permute-start.2 = (f32[16,3072]{1,0:T(8,128)S(1)}, f32[16,3072]{1,0:T(8,128)}, u32[]{:S(2)}, u32[]{:S(2)}) collective-permute-start(f32[16,3072]{1,0:T(8,128)S(1)} %fusion), channel_id=1, source_target_pairs={{0,3},{1,4},{2,5},{3,6},{4,7},{5,8},{6,9},{7,10},{8,11},{9,12},{10... | collective-permute-start | bytes 589832
  713.1 100.7 %collective-permute-start.1 = (f32[16,3072]{1,0:T(8,128)S(1)}, f32[16,3072]{1,0:T(8,128)}, u32[]{:S(2)}, u32[]{:S(2)}) collective-permute-start(f32[16,3072]{1,0:T(8,128)S(1)} %fusion), channel_id=1, source_target_pairs={{0,2},{1,3},{2,4},{3,5},{4,6},{5,7},{6,8},{7,9},{8,10},{9,11},{10,... | collective-permute-start | bytes 589832
  716.0 97.7 %collective-permute-start = (f32[16,3072]{1,0:T(8,128)S(1)}, f32[16,3072]{1,0:T(8,128)}, u32[]{:S(2)}, u32[]{:S(2)}) collective-permute-start(f32[16,3072]{1,0:T(8,128)S(1)} %fusion), channel_id=1, source_target_pairs={{0,1},{1,2},{2,3},{3,4},{4,5},{5,6},{6,7},{7,8},{8,9},{9,10},{10,1... | collective-permute-start | bytes 589832
  731.5 244.3 %all-reduce.10.cloned.1.call-start = ((), (), s32[]{:S(2)}) async-start(), calls=%async_computation.2 | async-start | bytes 393216 | tf_op jit(solution)/shard_map/psum | solution.py:112
  813.7 163.8 %all-gather.6.cloned.1.call-start = ((), (), s32[]{:S(2)}) async-start(), calls=%async_computation.3 | async-start | bytes 3342336 | tf_op jit(solution)/shard_map/all_gather | solution.py:111
  (59 other events, 1981.4 us)
Sparse Core Ops, SparseCore 0:
  9.7 57.9 all-gather.3
  731.7 81.9 all-reduce.7
  815.9 58.5 all-reduce.9
  900.2 48.5 all-gather.5
